TPU v7x, 128 devices: a whole 4x4x4 slice. The times are simulated.
128 devices in a mesh: donor: 4 (over y), var: 32 (over z, x, core).
Axes of the slice: x: 4, y: 4, z: 4, core: 2. Of those that a mesh axis runs over, the one named last changes fastest.
Arguments:
- genotype: bfloat16 [10240, 131072], P('donor', 'var'), may hold values from -20 to 20
- block_place: int32 [1024], P('var'), may hold values from 0 to 1023, each once
- expression: bfloat16 [10240, 256], P('donor', 'var'), may hold values from -80 to 80
- covariates: bfloat16 [10240, 64], P('donor'), may hold values from -5 to 5
- gene_start: int32 [256], replicated, may hold values from -26 to 1023, as said below
- gene_count: int32 [256], replicated, may hold values from 1 to 52, as said below
- membership: float32 [256, 12288], P('var'), may hold values from 0 to 1
Outputs:
- gene_pvalue: float32 [256], P('var')
- pathway_pvalue: float32 [12288], P('var')
Inputs may be any that keep to these rules, and one draw needn't show every extreme that they name: `block_place`: each genomic block is stored exactly once. gene_start[g] = 4 g - gene_count[g] // 2; window blocks outside 0 to 1023 hold no variants. `gene_count`: some gene has 52 blocks in every draw.
All inputs are finite; a program needn't handle non-finite values.
Results may differ from a plain program's by a relative error of at most 0.0057.
Values may be sent and summed in bfloat16 or wider, within the bound.
A program may use at most 192 MiB of HBM per device.

v0:
```python
import math

import jax
import jax.numpy as jnp
from jax import lax
from jax.sharding import PartitionSpec as P

BPG = 4
CMAX = 52
K = 64
GMAX = 14


EPSILON = 1e-06


def cauchy_terms(zscore):
    angle_value = 0.5 * math.pi * lax.erfc(jnp.abs(zscore) * (1.0 / math.sqrt(2.0)))
    return jnp.sign(zscore) * jnp.cos(angle_value) / jnp.sin(angle_value)


def solve_gram(gram_sum, right_side):
    factor = jnp.linalg.cholesky(gram_sum)
    middle = lax.linalg.triangular_solve(factor, right_side, left_side=True, lower=True)
    return lax.linalg.triangular_solve(factor, middle, left_side=True, lower=True, transpose_a=True)


def residualize(raw_values, cov_wide, beta_coef):
    return raw_values.astype(jnp.float32) - jnp.dot(
        cov_wide, beta_coef, precision=lax.Precision.HIGHEST
    )


def spread_to_genes(slot_sums, live_slots, safe_genes, genes_all):
    kept = jnp.where(live_slots, slot_sums, 0.0).reshape(-1)
    return jnp.zeros((genes_all,), jnp.float32).at[safe_genes.reshape(-1)].add(kept)


def local(genotype, block_place, expression, covariates, gene_start, gene_count, membership):
    don_rows, var_cols = genotype.shape
    blocks_here = block_place.shape[0]
    block_width = var_cols // blocks_here
    genes_all = gene_start.shape[0]
    genes_here = expression.shape[1]
    total_blocks = blocks_here * lax.axis_size("var")
    donors_all = don_rows * lax.axis_size("donor")
    cov_wide = covariates.astype(jnp.float32)
    gram_part = jnp.dot(covariates.T, covariates, preferred_element_type=jnp.float32)
    geno_part = jnp.dot(covariates.T, genotype, preferred_element_type=jnp.float32)
    expr_part = jnp.dot(covariates.T, expression, preferred_element_type=jnp.float32)
    gram_sum, geno_cross, expr_cross = lax.psum((gram_part, geno_part, expr_part), "donor")
    geno_res = residualize(genotype, cov_wide, solve_gram(gram_sum, geno_cross))
    expr_res = residualize(expression, cov_wide, solve_gram(gram_sum, expr_cross))
    geno_ss, expr_ss = lax.psum(
        (jnp.sum(geno_res * geno_res, axis=0), jnp.sum(expr_res * expr_res, axis=0)), "donor"
    )
    geno_std = (geno_res * lax.rsqrt(geno_ss + EPSILON)).astype(jnp.bfloat16)
    expr_std = (expr_res * lax.rsqrt(expr_ss + EPSILON)).astype(jnp.bfloat16)
    expr_all = lax.all_gather(expr_std, "var", axis=1, tiled=True)
    lead_blocks = CMAX - CMAX // 2 - 1
    offsets = jnp.arange(GMAX, dtype=jnp.int32)
    logical = block_place[:, None]
    slot_genes = jnp.floor_divide(logical - lead_blocks, BPG) + offsets[None, :]
    inside = (slot_genes >= 0) & (slot_genes < genes_all)
    safe_genes = jnp.clip(slot_genes, 0, genes_all - 1)
    window_start = gene_start[safe_genes]
    window_count = gene_count[safe_genes]
    live_slots = inside & (window_start <= logical) & (logical < window_start + window_count)
    picked = jnp.take(expr_all, safe_genes.reshape(-1), axis=1).reshape(don_rows, blocks_here, GMAX)
    geno_blocks = geno_std.reshape(don_rows, blocks_here, block_width)
    partial_value = jnp.einsum(
        "dbj,dbv->bjv", picked, geno_blocks, preferred_element_type=jnp.float32
    )
    scale_z = math.sqrt(donors_all - K - 2)
    whole_sums = lax.psum(partial_value, "donor")
    slot_sums = jnp.sum(cauchy_terms(whole_sums * scale_z), axis=2)
    gene_sum = lax.psum_scatter(
        spread_to_genes(slot_sums, live_slots, safe_genes, genes_all),
        "var",
        scatter_dimension=0,
        tiled=True,
    )
    first_gene = lax.axis_index("var") * genes_here
    own_start = lax.dynamic_slice_in_dim(gene_start, first_gene, genes_here)
    own_count = lax.dynamic_slice_in_dim(gene_count, first_gene, genes_here)
    covered = jnp.minimum(own_start + own_count, total_blocks) - jnp.maximum(own_start, 0)
    gene_stat = gene_sum / (block_width * covered).astype(jnp.float32)
    gene_pvalue = 0.5 - jnp.arctan(gene_stat) / math.pi
    path_part = jnp.dot(gene_stat, membership, precision=lax.Precision.HIGHEST)
    weight_part = jnp.sum(membership, axis=0)
    path_sum, path_weight = (
        lax.psum_scatter(path_part, "var", scatter_dimension=0, tiled=True),
        lax.psum_scatter(weight_part, "var", scatter_dimension=0, tiled=True),
    )
    pathway_pvalue = 0.5 - jnp.arctan(path_sum / jnp.maximum(path_weight, 1.0)) / math.pi
    return (gene_pvalue, pathway_pvalue)


def solution(mesh):
    placed = (
        P("donor", "var"),
        P("var"),
        P("donor", "var"),
        P("donor", None),
        P(),
        P(),
        P("var", None),
    )
    return jax.shard_map(
        local, mesh=mesh, in_specs=placed, out_specs=(P("var"), P("var")), check_vma=False
    )
```

profile of v0, /device:TPU:1, one launch (start us, length us, event | category | flops | bytes accessed | tf_op | source)
XLA Modules:
  0.0 406.6 jit_solution(12093813679113098288)
XLA Ops:
  7.2 0.9 copy-done
  8.1 11.7 %fusion.39 = f32[64,4096]{1,0:T(8,128)} fusion(bf16[2560,64]{0,1:T(8,128)(2,1)S(1)} %copy-done, bf16[2560,4096]{1,0:T(8,128)(2,1)} %param.8), kind=kOutput, calls=%fused_computation.83 | convolution fusion | flops 1342177280 | bytes 22347776 | tf_op jit(solution)/shard_map/dot_general | solution.py:49
  20.6 15.1 %all-reduce.5 = (f32[64,64]{0,1:T(8,128)S(1)}, f32[64,8]{0,1:T(8,128)S(1)}) all-reduce(f32[64,64]{0,1:T(8,128)S(1)} %fusion.37, f32[64,8]{0,1:T(8,128)S(1)} %fusion.38), channel_id=1, replica_groups=mesh['donor'=4,'var'=32] {'donor'}, use_global_device_ids=true, to_apply=%region_0.0 | all-reduce | flops 4608 | bytes 36864 | tf_op jit(solution)/shard_map/psum | solution.py:51
  35.8 5.8 %cholesky.18 = f32[64,64]{1,0:T(8,128)S(1)} custom-call(f32[64,64]{1,0:T(8,128)S(1)} %fusion.24), custom_call_target="Cholesky" | custom-call | tf_op jit(solution)/shard_map/jit(cholesky)/cholesky | solution.py:23
  41.7 0.6 compare_reduce_fusion
  42.3 0.7 fusion.15
  43.0 26.0 %copy.19 = bf16[2560,4096]{0,1:T(8,128)(2,1)} copy(bf16[2560,4096]{1,0:T(8,128)(2,1)} %param.8) | data formatting | bytes 41943040 | tf_op args[0]
  69.0 4.9 %custom-call.11 = f32[1,64,64]{1,2,0:T(8,128)S(1)} custom-call(f32[1,64,64]{2,1,0:T(8,128)S(1)} %fusion.15), custom_call_target="InvertDiagBlocksLowerTriangular" | custom-call | tf_op jit(solution)/shard_map/triangular_solve | solution.py:25
  74.5 0.4 multiply_reduce_fusion.1
  74.9 2.3 fusion.18
  77.1 1.0 fusion.16
  78.2 28.5 %multiply_reduce_fusion = (f32[4096]{0:T(1024)S(1)}, f32[4096,2560]{1,0:T(8,128)}) fusion(bf16[2560,4096]{0,1:T(8,128)(2,1)} %copy.19, f32[64,4096]{1,0:T(8,128)S(1)} %fusion.16, bf16[2560,64]{0,1:T(8,128)(2,1)S(1)} %copy-done), kind=kOutput, calls=%fused_computation.6 | convolution fusion | flops 8095002624 | bytes 64307200 | tf_op jit(solution)/shard_map/dot_general | solution.py:29
  106.6 10.9 %all-reduce.4 = (f32[4096]{0:T(1024)S(1)}, f32[8]{0:T(128)S(1)}) all-reduce(f32[4096]{0:T(1024)S(1)} %get-tuple-element.13, f32[8]{0:T(128)S(1)} %get-tuple-element.15), channel_id=1, replica_groups=mesh['donor'=4,'var'=32] {'donor'}, use_global_device_ids=true, to_apply=%region_8.10 | all-reduce | flops 4104 | bytes 32832 | tf_op jit(solution)/shard_map/psum | solution.py:54
  117.6 0.7 multiply_convert_fusion.1
  118.3 0.3 all-reduce.12.cloned.1.call-start
  118.6 27.4 %multiply_convert_fusion = bf16[2560,4096]{0,1:T(8,128)(2,1)} fusion(f32[4096,2560]{1,0:T(8,128)} %get-tuple-element.14, bf16[2560,4096]{0,1:T(8,128)(2,1)} %copy.19, f32[4096]{0:T(1024)S(1)} %add_rsqrt_fusion), kind=kLoop, calls=%fused_computation.5 | loop fusion | flops 41943040 | bytes 83902464 | tf_op jit(solution)/shard_map/convert_element_type | solution.py:57
  146.0 23.9 %all-gather.2.cloned.1.call-done = bf16[2560,256]{0,1:T(8,128)(2,1)} async-done(((bf16[2560,8]{0,1:T(8,128)(2,1)}), bf16[2560,256]{0,1:T(8,128)(2,1)}) %all-gather.2.cloned.1.call-update) | async-done | bytes 1310736 | tf_op jit(solution)/shard_map/all_gather | solution.py:59
  169.9 7.5 %gather_fusion.2 = bf16[448,2560]{1,0:T(8,128)(2,1)} fusion(bf16[2560,256]{0,1:T(8,128)(2,1)} %all-gather.2.cloned.1.call-done, s32[1024]{0:T(1024)S(1)} %pad_clamp_fusion), kind=kCustom, calls=%fused_computation.2 | custom fusion | bytes 4589312 | tf_op jit(solution)/shard_map/jit(_take)/gather | solution.py:69
  177.4 2.7 gather.21
  180.1 10.6 %fusion.1 = f32[32,14,128]{2,1,0:T(8,128)} fusion(bf16[2560,32,128]{0,2,1:T(8,128)(2,1)} %bitcast.53, bf16[2560,32,14]{0,2,1:T(8,128)(2,1)S(1)} %gather.21, pred[32,14]{1,0:T(8,128)(4,1)S(1)} %get-tuple-element.12), kind=kOutput, calls=%fused_computation.9 | convolution fusion | flops 294748160 | bytes 23495104 | tf_op jit(solution)/shard_map/dbj,dbv->bjv/dot_general | solution.py:71
  191.0 3.2 gather_fusion
  194.1 3.2 gather_fusion.1
  197.4 0.6 dynamic-slice
  198.7 0.7 reduce_sum.42
  199.4 29.8 %all-reduce.12.cloned.1.call-done = f32[32,14,128]{2,1,0:T(8,128)} async-done(((f32[32,14,128]{2,1,0:T(8,128)}), f32[32,14,128]{2,1,0:T(8,128)}) %all-reduce.12.cloned.1.call-update) | async-done | bytes 229392 | tf_op jit(solution)/shard_map/psum | solution.py:75
  229.2 2.6 fusion.14
  232.0 4.0 scatter_custom_fusion
  236.0 65.0 %all-reduce = f32[256]{0:T(256)S(1)} all-reduce(f32[256]{0:T(256)S(1)} %scatter_custom_fusion), channel_id=2, replica_groups=mesh['donor'=4,'var'=32] {'var'}, use_global_device_ids=true, to_apply=%region_12.14.clone | all-reduce | flops 256 | bytes 2048
  300.9 0.6 multiply_subtract_fusion.1
  301.6 1.1 fusion.32
  303.3 95.3 %all-reduce.14.cloned.1.call-done = (f32[12288]{0:T(1024)}, f32[12288]{0:T(1024)}) async-done(((f32[12288]{0:T(1024)}, f32[12288]{0:T(1024)}), (f32[12288]{0:T(1024)}, f32[12288]{0:T(1024)})) %all-reduce.14.cloned.1.call-update) | async-done | bytes 98320
  398.7 1.4 multiply_subtract_fusion
  (46 shorter events, 2.0 us)
Async XLA Ops:
  7.2 1.0 copy-start
  7.2 13.0 %copy-start.6 = (s32[32]{0:T(128)S(1)}, s32[32]{0:T(128)}, u32[]{:S(2)}) copy-start(s32[32]{0:T(128)} %param.9) | copy-start | bytes 388
  7.2 13.2 %copy-start.5 = (bf16[2560,8]{0,1:T(8,128)(2,1)S(1)}, bf16[2560,8]{0,1:T(8,128)(2,1)}, u32[]{:S(2)}) copy-start(bf16[2560,8]{0,1:T(8,128)(2,1)} %param.10) | copy-start | bytes 122884
  7.2 67.7 %all-reduce.10.cloned.1.call-start = ((), (), s32[]{:S(2)}) async-start(), calls=%async_computation.1 | async-start | bytes 2097152 | tf_op jit(solution)/shard_map/psum | solution.py:51
  19.9 150.0 %all-gather.2.cloned.1.call-start = ((), (), s32[]{:S(2)}) async-start(), calls=%async_computation | async-start | bytes 1351680 | tf_op jit(solution)/shard_map/all_gather | solution.py:59
  118.3 110.9 %all-reduce.12.cloned.1.call-start = ((), (), s32[]{:S(2)}) async-start(), calls=%async_computation.2 | async-start | bytes 524288 | tf_op jit(solution)/shard_map/psum | solution.py:75
  180.1 10.9 %copy-start.3 = (s32[256]{0:T(256)S(1)}, s32[256]{0:T(256)}, u32[]{:S(2)}) copy-start(s32[256]{0:T(256)} %param.12) | copy-start | bytes 3076
  180.1 14.1 %copy-start.2 = (s32[256]{0:T(256)S(1)}, s32[256]{0:T(256)}, u32[]{:S(2)}) copy-start(s32[256]{0:T(256)} %param.13) | copy-start | bytes 3076
  180.1 220.0 %copy-start.1 = (bf16[2560,64]{0,1:T(8,128)(2,1)S(1)}, bf16[2560,64]{0,1:T(8,128)(2,1)}, u32[]{:S(2)}) copy-start(bf16[2560,64]{0,1:T(8,128)(2,1)} %param.11) | copy-start | bytes 983044
  190.7 6.7 %copy-start.7 = (u32[128]{0:T(128)S(1)}, u32[128]{0:T(128)}, u32[]{:S(2)}) copy-start(u32[128]{0:T(128)} %constant.175) | copy-start | bytes 1540
  190.7 8.0 %copy-start.4 = (f32[8,12288]{1,0:T(8,128)S(1)}, f32[8,12288]{1,0:T(8,128)}, u32[]{:S(2)}) copy-start(f32[8,12288]{1,0:T(8,128)} %param.14) | copy-start | bytes 1179652
  190.7 207.9 %all-reduce.14.cloned.1.call-start = ((), (), s32[]{:S(2)}) async-start(), calls=%async_computation.3 | async-start | bytes 196608
Sparse Core Ops, SparseCore 0:
  20.0 47.8 all-reduce.9
  118.4 51.4 all-gather.1
  190.8 38.3 all-reduce.11
  302.8 95.8 all-reduce.13
where the time goes:
time: 408 us; the launch traced here: 407 us
  waiting for transfers between devices  149 us (37%)
  blocking collectives  91 us (22%)
  matrix products  56.2 us (14%)
  other arithmetic  49.9 us (12%)
  local copies, waits for them, and re-layouts  44.7 us (11%)
  between operations  15.3 us (4%)
    unnamed x5, waiting for transfers between devices  95.4 us
    unnamed x1, blocking collectives  65 us
    psum x1, waiting for transfers between devices, local(): whole_sums = lax.psum(partial_value, 'donor')  29.8 us
    dot_general x2, matrix products, residualize(): jnp.dot(cov_wide, beta_coef, precision=lax.Precision.HIGHEST)  28.9 us
    unnamed x18, local copies, waits for them, and re-layouts  27.5 us
    convert_element_type x1, other arithmetic, local(): geno_std = (geno_res * lax.rsqrt(geno_ss + EPSILON)).astype(jnp.bfloat16)  27.4 us
    all_gather x1, waiting for transfers between devices, local(): expr_all = lax.all_gather(expr_std, 'var', axis=1, tiled=True)  23.9 us
    psum x1, blocking collectives, local(): lax.psum((gram_part, geno_part, expr_part), 'donor')  15.1 us
  transfers between devices with their start and end apart: 4, of which 3 were waited for; matrix products, arithmetic and copies ran while one was open for 18% of the time, Pallas kernels for 0%

commit v1 on v0

v1 whole, which is shorter than its diff:
```python
import math

import jax
import jax.numpy as jnp
from jax import lax
from jax.experimental import pallas as pl
from jax.experimental.pallas import tpu as pltpu
from jax.sharding import PartitionSpec as P

BPG = 4
CMAX = 52
K = 64
GMAX = 14
VB = 128
EPSILON = 1e-06
HIGHEST = lax.Precision.HIGHEST
MESH = pl.DeviceIdType.MESH
LEAD = CMAX - CMAX // 2 - 1
PAD = 8
ROWS = 72
TILE = 256


def cauchy_terms(zscore):
    angle_value = 0.5 * math.pi * lax.erfc(jnp.abs(zscore) * (1.0 / math.sqrt(2.0)))
    return jnp.sign(zscore) * jnp.cos(angle_value) / jnp.sin(angle_value)


def iota(shape, dim):
    return lax.broadcasted_iota(jnp.int32, shape, dim)


def sweep(pivot, mat):
    shape = mat.shape
    on_row = iota(shape, 0) == pivot
    on_col = iota(shape, 1) == pivot
    row = jnp.sum(jnp.where(on_row, mat, 0.0), axis=0, keepdims=True)
    col = jnp.sum(jnp.where(on_col, mat, 0.0), axis=1, keepdims=True)
    here = iota((shape[0], 1), 0) == pivot
    value = jnp.sum(jnp.where(here, col, 0.0), axis=0, keepdims=True)
    row = jnp.where(iota((1, shape[1]), 1) == pivot, 1.0, row) * (1.0 / value)
    col = jnp.where(here, 0.0, col)
    return jnp.where(on_row, row, jnp.where(on_col, 0.0, mat) - col * row)


def correlate(
    donors, groups, ce_ref, place_ref, x_ref, member_ref, out_ref, members_ref,
    xv, ct, ccc, small, inv_ref, cross_out, cross_in, beta, slab, expr_t, geno, pieces, wide, slot_out, slot_in,
    x_sem, small_sent, small_got, cross_sent, cross_got, beta_sent, beta_got,
    slab_sent, slab_got, member_sent, member_got, own_sem, slot_sent, slot_got,
):
    my_donor = lax.axis_index("donor")
    my_var = lax.axis_index("var")
    don_rows = ce_ref.shape[0]
    cols = xv.shape[2]
    tiles = cols // TILE
    chunks = don_rows // TILE
    paths = members_ref.shape[1]
    genes_here = member_ref.shape[0]
    half = slab.shape[2]

    def donor_at(step):
        return lax.rem(my_donor + step, donors)

    def var_at(step):
        return lax.rem(my_var + step, groups)

    def load(turn):
        start = pl.multiple_of(donor_at(1 + turn) * cols, cols)
        return pltpu.make_async_copy(x_ref.at[:, pl.ds(start, cols)], xv.at[turn], x_sem.at[turn])

    for turn in range(donors):
        load(turn).start()

    barrier = pltpu.get_barrier_semaphore()
    for step in range(1, donors):
        pl.semaphore_signal(
            barrier, inc=1, device_id=(donor_at(step), my_var), device_id_type=MESH
        )

    def greet(step, carry):
        pl.semaphore_signal(
            barrier, inc=1, device_id=(my_donor, var_at(step)), device_id_type=MESH
        )
        return carry

    lax.fori_loop(1, groups, greet, 0)

    eye = (iota((128, 128), 0) == iota((128, 128), 1)).astype(jnp.bfloat16)
    thrice = (iota((128, 256), 0) == lax.rem(iota((128, 256), 1), K)).astype(jnp.bfloat16)

    def prepare(chunk, total):
        rows = pl.ds(pl.multiple_of(chunk * TILE, TILE), TILE)
        part = ce_ref[rows, :]
        flipped = lax.dot_general(
            eye, part, (((1,), (1,)), ((), ())), preferred_element_type=jnp.float32
        ).astype(jnp.bfloat16)
        ct[:, rows] = flipped
        ccc[rows, :] = jnp.dot(part, thrice, preferred_element_type=jnp.float32).astype(
            jnp.bfloat16
        )
        return total + jnp.dot(flipped, part, preferred_element_type=jnp.float32)

    small[my_donor] = lax.fori_loop(0, chunks, prepare, jnp.zeros((128, 128), jnp.float32))
    pl.semaphore_wait(barrier, donors + groups - 2)

    def to_donor(step, src, dst, sent, got):
        return pltpu.make_async_remote_copy(
            src_ref=src,
            dst_ref=dst.at[my_donor],
            send_sem=sent.at[step],
            recv_sem=got.at[my_donor],
            device_id=(donor_at(step), my_var),
            device_id_type=MESH,
        )

    def from_donor(step, dst, sent, got):
        peer = donor_at(step)
        return pltpu.make_async_remote_copy(
            src_ref=dst.at[peer],
            dst_ref=dst.at[peer],
            send_sem=sent.at[step],
            recv_sem=got.at[peer],
            device_id=(peer, my_var),
            device_id_type=MESH,
        )

    for step in range(1, donors):
        to_donor(step, small.at[my_donor], small, small_sent, small_got).start()

    def member_copy(step):
        peer = var_at(step)
        return pltpu.make_async_remote_copy(
            src_ref=member_ref.at[:, pl.ds(pl.multiple_of(peer * paths, 128), paths)],
            dst_ref=members_ref.at[pl.ds(pl.multiple_of(my_var * genes_here, 8), genes_here), :],
            send_sem=member_sent.at[step],
            recv_sem=member_got.at[my_var],
            device_id=(my_donor, peer),
            device_id_type=MESH,
        )

    def member_back(step):
        peer = var_at(step)
        rows = members_ref.at[pl.ds(pl.multiple_of(peer * genes_here, 8), genes_here), :]
        return pltpu.make_async_remote_copy(
            src_ref=rows,
            dst_ref=rows,
            send_sem=member_sent.at[step],
            recv_sem=member_got.at[peer],
            device_id=(my_donor, peer),
            device_id_type=MESH,
        )

    def each(first, last, act):
        def body(step, carry):
            act(step)
            return carry

        lax.fori_loop(first, last, body, 0)

    each(1, groups, lambda step: member_copy(step).start())
    own_member = pltpu.make_async_copy(
        member_ref.at[:, pl.ds(pl.multiple_of(my_var * paths, 128), paths)],
        members_ref.at[pl.ds(pl.multiple_of(my_var * genes_here, 8), genes_here), :],
        own_sem,
    )
    own_member.start()

    wide[...] = jnp.zeros_like(wide)
    for step in range(1, donors):
        from_donor(step, small, small_sent, small_got).wait_recv()
    sums = small[0]
    for donor in range(1, donors):
        sums = sums + small[donor]

    def moments(turn, steps_done, sweeping):
        def body(index, carry):
            if sweeping:
                carry = sweep(steps_done + index, carry)
            tile = lax.div(index, chunks)
            chunk = lax.rem(index, chunks)
            rows = pl.ds(pl.multiple_of(chunk * TILE, TILE), TILE)
            lanes = pl.ds(pl.multiple_of(tile * TILE, TILE), TILE)
            part = xv[turn, rows, lanes]
            product = jnp.dot(ct[0:K, rows], part, preferred_element_type=jnp.float32)
            part = part.astype(jnp.float32)
            square = jnp.sum((part * part).reshape(TILE // 8, 8, TILE), axis=0)
            fresh = chunk == 0
            cross_out[turn, 0:K, lanes] = product + jnp.where(
                fresh, 0.0, cross_out[turn, 0:K, lanes]
            )
            cross_out[turn, K:ROWS, lanes] = square + jnp.where(
                fresh, 0.0, cross_out[turn, K:ROWS, lanes]
            )
            return carry

        return body

    mat = jnp.where(iota((K, 128), 1) < K, sums[0:K, :], 0.0)
    done = 0
    for turn in range(donors):
        load(turn).wait()
        now = min(K - done, tiles * chunks)
        mat = lax.fori_loop(0, now, moments(turn, done, True), mat)
        mat = lax.fori_loop(now, tiles * chunks, moments(turn, done, False), mat)
        done += now
        if turn < donors - 1:
            to_donor(turn + 1, cross_out.at[turn], cross_in, cross_sent, cross_got).start()
        else:
            cross_in[my_donor] = cross_out[turn]
    inv_ref[...] = mat
    inverse = inv_ref[:, 0:K]

    expr_rows = sums[K : K + 8, :]
    expr_coef = jnp.dot(
        expr_rows[:, 0:K], mat, precision=HIGHEST, preferred_element_type=jnp.float32
    )
    on_diag = iota((8, 128), 1) == iota((8, 128), 0) + K
    expr_sq = jnp.sum(jnp.where(on_diag, expr_rows, 0.0), axis=1, keepdims=True)
    in_cov = iota((8, 128), 1) < K
    expr_ss = expr_sq - jnp.sum(jnp.where(in_cov, expr_rows * expr_coef, 0.0), axis=1, keepdims=True)
    expr_scale = lax.rsqrt(jnp.maximum(expr_ss, 0.0) + EPSILON)
    mixing = jnp.where(in_cov, -expr_coef, jnp.where(on_diag, 1.0, 0.0))
    halves = []
    for part in range(2):
        resid = jnp.dot(
            mixing,
            ct[:, part * half : (part + 1) * half].astype(jnp.float32),
            precision=HIGHEST,
            preferred_element_type=jnp.float32,
        )
        halves.append(resid * expr_scale)
    slab[my_var] = jnp.concatenate(halves, axis=0).astype(jnp.bfloat16)

    def slab_copy(step):
        peer = var_at(step)
        return pltpu.make_async_remote_copy(
            src_ref=slab.at[my_var],
            dst_ref=slab.at[my_var],
            send_sem=slab_sent.at[step],
            recv_sem=slab_got.at[my_var],
            device_id=(my_donor, peer),
            device_id_type=MESH,
        )

    def slab_back(step):
        peer = var_at(step)
        return pltpu.make_async_remote_copy(
            src_ref=slab.at[peer],
            dst_ref=slab.at[peer],
            send_sem=slab_sent.at[step],
            recv_sem=slab_got.at[peer],
            device_id=(my_donor, peer),
            device_id_type=MESH,
        )

    each(1, groups, lambda step: slab_copy(step).start())

    for step in range(1, donors):
        from_donor(step, cross_in, cross_sent, cross_got).wait_recv()

    def solve(tile, carry):
        lanes = pl.ds(pl.multiple_of(tile * TILE, TILE), TILE)
        total = cross_in[0, :, lanes]
        for donor in range(1, donors):
            total = total + cross_in[donor, :, lanes]
        cross = total[0:K, :]
        square = jnp.sum(total[K:ROWS, :], axis=0, keepdims=True)
        coef = jnp.dot(
            inverse, cross, precision=HIGHEST, preferred_element_type=jnp.float32
        )
        left = square - jnp.sum(cross * coef, axis=0, keepdims=True)
        scale = lax.rsqrt(jnp.maximum(left, 0.0) + EPSILON)
        beta[my_donor, 0:K, lanes] = coef * scale
        beta[my_donor, K:ROWS, lanes] = jnp.broadcast_to(scale, (ROWS - K, TILE))
        return carry

    lax.fori_loop(0, tiles, solve, 0)
    for step in range(1, donors):
        to_donor(step, beta.at[my_donor], beta, beta_sent, beta_got).start()

    each(1, groups, lambda step: slab_back(step).wait_recv())
    per_copy = 4

    def unfold(index, carry):
        first = pl.multiple_of(index * per_copy, per_copy)
        part = slab[pl.ds(first, per_copy)].astype(jnp.float32)
        rows = pl.ds(pl.multiple_of(first * 8, per_copy * 8), per_copy * 8)
        expr_t[rows, 0:half] = part[:, 0:8, :].reshape(per_copy * 8, half).astype(jnp.bfloat16)
        expr_t[rows, half : 2 * half] = (
            part[:, 8:16, :].reshape(per_copy * 8, half).astype(jnp.bfloat16)
        )
        return carry

    lax.fori_loop(0, groups // per_copy, unfold, 0)

    def quarter(step):
        owner = donor_at(step)
        turn = (step + donors - 1) % donors

        def one_tile(tile, carry):
            lanes = pl.ds(pl.multiple_of(tile * TILE, TILE), TILE)
            coef = beta[owner, 0:K, lanes]
            scale = beta[owner, K : K + 1, lanes]
            for piece in range(3):
                rounded = coef.astype(jnp.bfloat16)
                pieces[piece * K : (piece + 1) * K, :] = rounded
                coef = coef - rounded.astype(jnp.float32)

            def standardize(chunk, inner):
                rows = pl.ds(pl.multiple_of(chunk * TILE, TILE), TILE)
                fitted = jnp.dot(
                    ccc[rows, 0 : 3 * K], pieces[...], preferred_element_type=jnp.float32
                )
                part = xv[turn, rows, lanes].astype(jnp.float32)
                geno[rows, :] = (part * scale - fitted).astype(jnp.bfloat16)
                return inner

            lax.fori_loop(0, chunks, standardize, 0)
            found = jnp.dot(expr_t[...], geno[...], preferred_element_type=jnp.float32)
            for side in range(TILE // VB):
                wide[side, PAD : PAD + expr_t.shape[0], :] = found[:, side * VB : (side + 1) * VB]
            for side in range(TILE // VB):
                block = tile * (TILE // VB) + side
                place = place_ref[owner * (cols // VB) + block]
                base = jnp.right_shift(place - LEAD, 2) + PAD
                found = wide[side, pl.ds(base, 16), :]
                if step:
                    slot_out[step, block] = found
                else:
                    slot_in[my_donor, block] = found
            return carry

        lax.fori_loop(0, tiles, one_tile, 0)

    for step in (0, 1, 3, 2):
        if step:
            from_donor(step, beta, beta_sent, beta_got).wait_recv()
        quarter(step)
        if step:
            to_donor(step, slot_out.at[step], slot_in, slot_sent, slot_got).start()

    for step in range(1, donors):
        from_donor(step, slot_in, slot_sent, slot_got).wait_recv()
    total = slot_in[0]
    for donor in range(1, donors):
        total = total + slot_in[donor]
    out_ref[...] = total

    own_member.wait()
    each(1, groups, lambda step: member_back(step).wait_recv())
    each(1, groups, lambda step: member_copy(step).wait_send())
    each(1, groups, lambda step: slab_copy(step).wait_send())
    for step in range(1, donors):
        to_donor(step, small.at[my_donor], small, small_sent, small_got).wait_send()
        to_donor(step, cross_out.at[step - 1], cross_in, cross_sent, cross_got).wait_send()
        to_donor(step, beta.at[my_donor], beta, beta_sent, beta_got).wait_send()
        to_donor(step, slot_out.at[step], slot_in, slot_sent, slot_got).wait_send()


def add_all(donors, groups, x_ref, out_ref, near, far, near_sent, near_got, far_sent, far_got):
    my_donor = lax.axis_index("donor")
    my_var = lax.axis_index("var")
    my_core = lax.rem(my_var, 2)
    my_chip = lax.div(my_var, 2)
    near_count, far_count = donors * 2, groups // 2
    my_near = my_donor * 2 + my_core

    def near_id(step):
        place = lax.rem(my_near + step, near_count)
        return place, (lax.div(place, 2), my_chip * 2 + lax.rem(place, 2))

    def far_id(step):
        place = lax.rem(my_chip + step, far_count)
        return place, (my_donor, place * 2 + my_core)

    barrier = pltpu.get_barrier_semaphore()
    for step in range(1, near_count):
        pl.semaphore_signal(barrier, inc=1, device_id=near_id(step)[1], device_id_type=MESH)
    for step in range(1, far_count):
        pl.semaphore_signal(barrier, inc=1, device_id=far_id(step)[1], device_id_type=MESH)
    near[my_near] = x_ref[...]
    pl.semaphore_wait(barrier, near_count + far_count - 2)

    for buffer, mine, count, where, sent, got in (
        (near, my_near, near_count, near_id, near_sent, near_got),
        (far, my_chip, far_count, far_id, far_sent, far_got),
    ):
        copies = []
        for step in range(1, count):
            copy = pltpu.make_async_remote_copy(
                src_ref=buffer.at[mine],
                dst_ref=buffer.at[mine],
                send_sem=sent.at[step],
                recv_sem=got.at[mine],
                device_id=where(step)[1],
                device_id_type=MESH,
            )
            copy.start()
            copies.append(copy)
        for step in range(1, count):
            peer, device = where(step)
            pltpu.make_async_remote_copy(
                src_ref=buffer.at[peer],
                dst_ref=buffer.at[peer],
                send_sem=sent.at[step],
                recv_sem=got.at[peer],
                device_id=device,
                device_id_type=MESH,
            ).wait_recv()
        total = buffer[0]
        for index in range(1, count):
            total = total + buffer[index]
        if buffer is near:
            far[my_chip] = total
        else:
            out_ref[...] = total
        for copy in copies:
            copy.wait_send()


def local(genotype, block_place, expression, covariates, gene_start, gene_count, membership):
    don_rows, var_cols = genotype.shape
    blocks_here = block_place.shape[0]
    block_width = var_cols // blocks_here
    genes_all = gene_start.shape[0]
    genes_here = expression.shape[1]
    groups = lax.axis_size("var")
    donors = lax.axis_size("donor")
    total_blocks = blocks_here * groups
    donors_all = don_rows * donors
    paths_here = membership.shape[1] // groups
    cols = var_cols // donors
    blocks_own = blocks_here // donors

    ce = jnp.concatenate(
        [
            covariates,
            expression,
            jnp.zeros((don_rows, 128 - K - genes_here), jnp.bfloat16),
        ],
        axis=1,
    )
    vmem = pl.BlockSpec(memory_space=pltpu.VMEM)
    anywhere = pl.BlockSpec(memory_space=pl.ANY)
    dma = pltpu.SemaphoreType.DMA

    def body(*refs):
        correlate(donors, groups, *refs)

    slots, members = pl.pallas_call(
        body,
        out_shape=(
            jax.ShapeDtypeStruct((blocks_own, 16, VB), jnp.float32),
            jax.ShapeDtypeStruct((genes_all, paths_here), jnp.float32),
        ),
        in_specs=[vmem, pl.BlockSpec(memory_space=pltpu.SMEM), anywhere, anywhere],
        out_specs=(vmem, vmem),
        scratch_shapes=[
            pltpu.VMEM((donors, don_rows, cols), jnp.bfloat16),
            pltpu.VMEM((128, don_rows), jnp.bfloat16),
            pltpu.VMEM((don_rows, 256), jnp.bfloat16),
            pltpu.VMEM((donors, 128, 128), jnp.float32),
            pltpu.VMEM((K, 128), jnp.float32),
            pltpu.VMEM((donors, ROWS, cols), jnp.float32),
            pltpu.VMEM((donors, ROWS, cols), jnp.float32),
            pltpu.VMEM((donors, ROWS, cols), jnp.float32),
            pltpu.VMEM((groups, 16, don_rows // 2), jnp.bfloat16),
            pltpu.VMEM((genes_all, don_rows), jnp.bfloat16),
            pltpu.VMEM((don_rows, TILE), jnp.bfloat16),
            pltpu.VMEM((3 * K, TILE), jnp.bfloat16),
            pltpu.VMEM((TILE // VB, genes_all + 24, VB), jnp.float32),
            pltpu.VMEM((donors, blocks_own, 16, VB), jnp.float32),
            pltpu.VMEM((donors, blocks_own, 16, VB), jnp.float32),
            dma((donors,)),
            *[dma((donors,)) for _ in range(6)],
            *[dma((groups,)) for _ in range(4)],
            dma,
            *[dma((donors,)) for _ in range(2)],
        ],
        compiler_params=pltpu.CompilerParams(
            collective_id=0, has_side_effects=True, vmem_limit_bytes=56 * 2**20
        ),
        name="correlate",
    )(ce, block_place, genotype, membership)

    place_own = lax.dynamic_slice_in_dim(
        block_place, lax.axis_index("donor") * blocks_own, blocks_own
    )
    offsets = jnp.arange(GMAX, dtype=jnp.int32)
    logical = place_own[:, None]
    slot_genes = jnp.floor_divide(logical - LEAD, BPG) + offsets[None, :]
    corr = slots[:, :GMAX, :]
    slot_sums = jnp.sum(cauchy_terms(corr * math.sqrt(donors_all - K - 2)), axis=2)
    genes = jnp.arange(genes_all, dtype=jnp.int32)
    hot = slot_genes[:, :, None] == genes
    live = (gene_start <= logical) & (logical < gene_start + gene_count)
    hot = hot & live[:, None, :]
    gene_part = jnp.sum(jnp.where(hot, slot_sums[:, :, None], 0.0), axis=(0, 1))

    def total_body(*refs):
        add_all(donors, groups, *refs)

    gene_sum = pl.pallas_call(
        total_body,
        out_shape=jax.ShapeDtypeStruct((genes_all // 128, 128), jnp.float32),
        in_specs=[vmem],
        out_specs=vmem,
        scratch_shapes=[
            pltpu.VMEM((donors * 2, genes_all // 128, 128), jnp.float32),
            pltpu.VMEM((groups // 2, genes_all // 128, 128), jnp.float32),
            dma((donors * 2,)),
            dma((donors * 2,)),
            dma((groups // 2,)),
            dma((groups // 2,)),
        ],
        compiler_params=pltpu.CompilerParams(collective_id=1, has_side_effects=True),
        name="add_all",
    )(gene_part.reshape(genes_all // 128, 128)).reshape(-1)

    covered = jnp.minimum(gene_start + gene_count, total_blocks) - jnp.maximum(gene_start, 0)
    gene_stat = gene_sum / (block_width * covered).astype(jnp.float32)
    own_stat = lax.dynamic_slice_in_dim(
        gene_stat, lax.axis_index("var") * genes_here, genes_here
    )
    gene_pvalue = 0.5 - jnp.arctan(own_stat) / math.pi
    path_sum = jnp.dot(gene_stat, members, precision=HIGHEST)
    path_weight = jnp.sum(members, axis=0)
    pathway_pvalue = 0.5 - jnp.arctan(path_sum / jnp.maximum(path_weight, 1.0)) / math.pi
    return (gene_pvalue, pathway_pvalue)


def solution(mesh):
    placed = (
        P("donor", "var"),
        P("var"),
        P("donor", "var"),
        P("donor", None),
        P(),
        P(),
        P("var", None),
    )
    return jax.shard_map(
        local, mesh=mesh, in_specs=placed, out_specs=(P("var"), P("var")), check_vma=False
    )
```

time: 408 us -> 129 us (0.32)
  waiting for transfers between devices: 149 us -> 0 us
  Pallas kernels: 0 us -> 118 us
  blocking collectives: 91 us -> 0 us
  matrix products: 56.2 us -> 1.31 us
  other arithmetic: 49.9 us -> 6.4 us
  local copies, waits for them, and re-layouts: 44.7 us -> 2.57 us
  between operations: 15.3 us -> 0.7 us
    pallas_call x0 -> x2, Pallas kernels: none -> 118 us  [the longest x1 104 us: local(): pl.pallas_call(body, out_shape=(jax.ShapeDtypeStruct((blocks_own, 16, VB)...]
    unnamed x5 -> x0, waiting for transfers between devices: 95.4 us -> none
    unnamed x1 -> x0, blocking collectives: 65 us -> none
    dot_general x7 -> x1, matrix products: 52.7 us -> 1.31 us  [local(): path_sum = jnp.dot(gene_stat, members, precision=HIGHEST)]
    psum x2 -> x0, waiting for transfers between devices: 29.8 us -> none  [the longest x1 29.8 us: local(): whole_sums = lax.psum(partial_value, 'donor')]
    convert_element_type x2 -> x0, other arithmetic: 28.1 us -> none  [the longest x1 27.4 us: local(): geno_std = (geno_res * lax.rsqrt(geno_ss + EPSILON)).astype(jnp.bfloat16)]
    psum x2 -> x0, blocking collectives: 26 us -> none  [the longest x1 15.1 us: local(): lax.psum((gram_part, geno_part, expr_part), 'donor')]
    unnamed x18 -> x8, local copies, waits for them, and re-layouts: 27.5 us -> 2.41 us
  transfers between devices with their start and end apart: 4 -> 0, of which waited for: 3 -> 0; matrix products, arithmetic and copies ran while one was open for 18% -> 0% of each run, Pallas kernels for 0% -> 0%
where the time goes in v1:
time: 129 us
  Pallas kernels  118 us (91%)
  other arithmetic  6.4 us (5%)
  local copies, waits for them, and re-layouts  2.57 us (2%)
  matrix products  1.31 us (1%)
    pallas_call x1, Pallas kernels, local(): pl.pallas_call(body, out_shape=(jax.ShapeDtypeStruct((blocks_own, 16, VB)...  104 us
    pallas_call x1, Pallas kernels, local(): pl.pallas_call(total_body, out_shape=jax.ShapeDtypeStruct((genes_all // 1...  13.5 us

profile of v1, /device:TPU:1, one launch (start us, length us, event | category | flops | bytes accessed | tf_op | source)
XLA Modules:
  0.0 128.9 jit_solution(3909392632363648598)
XLA Ops:
  0.6 1.1 copy.14
  1.7 1.3 %copy.13 = bf16[2560,64]{1,0:T(8,128)(2,1)S(1)} copy(bf16[2560,64]{0,1:T(8,128)(2,1)} %param.10) | data formatting | bytes 655360 | tf_op args[3]
  3.1 0.1 pad.2.clone
  3.1 1.2 maximum_maximum_fusion.refs_0_
  4.4 0.0 copy-start.1
  4.4 0.0 copy-start
  4.4 0.0 copy-start.2
  4.4 104.4 %correlate.1 = (f32[8,16,128]{2,1,0:T(8,128)}, f32[256,384]{1,0:T(8,128)}) custom-call(bf16[2560,128]{1,0:T(8,128)(2,1)} %maximum_maximum_fusion.refs_0_, s32[32]{0:T(128)} %refs_1_.1, bf16[2560,4096]{1,0:T(8,128)(2,1)} %refs_2_.1, f32[8,12288]{1,0:T(8,128)} %refs_3_.1), custom_call_target="tpu_custom_call" | custom-call | tf_op jit(solution)/shard_map/correlate/pallas_call | solution.py:451
  108.8 1.3 %fusion.10 = f32[8,14]{1,0:T(8,128)S(1)} fusion(f32[8,16,128]{2,1,0:T(8,128)} %get-tuple-element.4), kind=kLoop, calls=%fused_computation.25 | loop fusion | flops 974736 | bytes 57792 | tf_op jit(solution)/shard_map/reduce_sum | solution.py:494
  110.1 0.1 copy.15
  110.2 0.0 copy-done.1
  110.2 0.1 and_select_fusion
  110.3 0.0 copy-done
  110.3 0.0 copy-done.2
  110.3 0.1 compare_and_fusion
  110.4 0.7 select_reduce_fusion
  111.1 13.5 %add_all.1 = f32[2,128]{1,0:T(2,128)} custom-call(f32[2,128]{1,0:T(2,128)} %bitcast.7), custom_call_target="tpu_custom_call" | custom-call | tf_op jit(solution)/shard_map/add_all/pallas_call | solution.py:504
  124.6 0.7 bitcast_divide_fusion
  125.3 0.6 multiply_subtract_fusion.1
  125.9 1.3 %convolution_reduce_fusion = f32[384]{0:T(512)S(1)} fusion(f32[256,1]{0,1:T(1,128)S(1)} %bitcast.6, f32[256,384]{1,0:T(8,128)} %get-tuple-element.5), kind=kOutput, calls=%fused_computation | convolution fusion | flops 1179648 | bytes 395776 | tf_op jit(solution)/shard_map/dot_general | solution.py:527
  127.2 1.0 reduce_sum.29
  128.3 0.6 multiply_subtract_fusion
  (3 shorter events, 0.0 us)
Async XLA Ops:
  4.4 105.8 %copy-start.1 = (s32[32]{0:T(128)S(1)}, s32[32]{0:T(128)}, u32[]{:S(2)}) copy-start(s32[32]{0:T(128)} %refs_1_.1) | copy-start | bytes 388
  4.4 105.9 %copy-start = (s32[256]{0:T(256)S(1)}, s32[256]{0:T(256)}, u32[]{:S(2)}) copy-start(s32[256]{0:T(256)} %param.11) | copy-start | bytes 3076
  4.4 105.9 %copy-start.2 = (s32[256]{0:T(256)S(1)}, s32[256]{0:T(256)}, u32[]{:S(2)}) copy-start(s32[256]{0:T(256)} %param.12) | copy-start | bytes 3076

commit v2 on v1

v2 whole, which is shorter than its diff:
```python
import math

import jax
import jax.numpy as jnp
from jax import lax
from jax.experimental import pallas as pl
from jax.experimental.pallas import tpu as pltpu
from jax.sharding import PartitionSpec as P

BPG = 4
CMAX = 52
K = 64
GMAX = 14
VB = 128
EPSILON = 1e-06
HIGHEST = lax.Precision.HIGHEST
MESH = pl.DeviceIdType.MESH
LEAD = CMAX - CMAX // 2 - 1
PAD = 8
ROWS = 72
TILE = 256
STRIP = 512


SIN = (1.6059043837e-10, -2.5052108385e-8, 2.7557319224e-6, -1.9841269841e-4, 8.3333333333e-3, -1.6666666667e-1, 1.0)
COS = (-1.1470745598e-11, 2.0876756988e-9, -2.7557319224e-7, 2.4801587302e-5, -1.3888888889e-3, 4.1666666667e-2, -0.5, 1.0)
ERF = (7.853861353153693e-5, -8.010193625184903e-4, 5.188327685732524e-3, -2.685381193529856e-2, 1.128358514861418e-1, -3.761262582423300e-1, 1.128379165726710)
ERFC_MID = (2.326819970068386e-2, -1.387039388740657e-1, 3.687424674597105e-1, -5.824733027278666e-1, 6.210004621745983e-1, -4.944515323274145e-1, 3.404879937665872e-1, -2.741127028184656e-1, 5.638259427386472e-1)
ERFC_FAR = (-1.047766399936249e1, 1.297719955372516e1, -7.495518717768503, 2.921019019210786, -1.015265279202700, 4.218463358204948e-1, -2.820767439740514e-1, 5.641895067754075e-1)
ATAN = (8.05374449538e-2, -1.38776856032e-1, 1.99777106478e-1, -3.33329491539e-1)


def poly(value, coefs):
    total = jnp.full_like(value, coefs[0])
    for coef in coefs[1:]:
        total = total * value + coef
    return total


def erfc(value):
    square = value * value
    inner = 1.0 - value * poly(square, ERF)
    safe = jnp.maximum(value, 0.5)
    recip = 1.0 / safe
    back = recip * recip
    outer = jnp.exp(-square) * recip * jnp.where(value < 2.0, poly(back, ERFC_MID), poly(back, ERFC_FAR))
    return jnp.where(value < 1.0, inner, outer)


def arctan(value):
    size = jnp.abs(value)
    big, mid = size > 2.414213562373095, size > 0.4142135623730950
    inner = jnp.where(big, -1.0 / jnp.maximum(size, 1.0), jnp.where(mid, (size - 1.0) / (size + 1.0), size))
    base = jnp.where(big, 0.5 * math.pi, jnp.where(mid, 0.25 * math.pi, 0.0))
    square = inner * inner
    result = base + (poly(square, ATAN) * square * inner + inner)
    return jnp.where(value < 0.0, -result, result)


def steps_of(values):
    largest = jnp.max(jnp.abs(values), axis=0, keepdims=True)
    scaled = values * (32767.0 / jnp.maximum(largest, 1e-30))
    return jnp.floor(scaled + 0.5).astype(jnp.int32).astype(jnp.int16), largest * (1.0 / 32767.0)


def two_rows(first, second):
    row = iota((8, first.shape[1]), 0)
    return jnp.where(row == 0, first, jnp.where(row == 1, second, 0.0))


def diagonal(mat):
    on_diag = iota(mat.shape, 0) == iota(mat.shape, 1)
    return jnp.sum(jnp.where(on_diag, mat, 0.0), axis=1, keepdims=True)


def cauchy_terms(zscore):
    angle = 0.5 * math.pi * erfc(jnp.abs(zscore) * (1.0 / math.sqrt(2.0)))
    square = angle * angle
    sign = jnp.where(zscore > 0.0, 1.0, jnp.where(zscore < 0.0, -1.0, 0.0))
    return sign * poly(square, COS) / (angle * poly(square, SIN))


def iota(shape, dim):
    return lax.broadcasted_iota(jnp.int32, shape, dim)


def sweep(pivot, mat):
    shape = mat.shape
    on_row = iota(shape, 0) == pivot
    on_col = iota(shape, 1) == pivot
    row = jnp.sum(jnp.where(on_row, mat, 0.0), axis=0, keepdims=True)
    col = jnp.sum(jnp.where(on_col, mat, 0.0), axis=1, keepdims=True)
    here = iota((shape[0], 1), 0) == pivot
    value = jnp.sum(jnp.where(here, col, 0.0), axis=0, keepdims=True)
    row = jnp.where(iota((1, shape[1]), 1) == pivot, 1.0, row) * (1.0 / value)
    col = jnp.where(here, 0.0, col)
    return jnp.where(on_row, row, jnp.where(on_col, 0.0, mat) - col * row)


def correlate(
    donors, groups, total_blocks, ct_ref, et_ref, place_ref, start_ref, count_ref, x_ref, member_ref, gene_ref, path_ref,
    members_ref, xv, ct, ccc, small, inv_ref, cross_out, sides_out, cross_in, sides_in, beta, beta_sides, slab, expr_t, expr_sums, pieces, wide,
    slot_out, slot_in, near, far,
    x_sem, small_sent, small_got, cross_sent, cross_got, sides_sent, sides_got, beta_sent, beta_got, scale_sent, scale_got, expr_sent, expr_got, slot_sent, slot_got,
    slab_sent, slab_got, member_sent, member_got, own_sem, near_sent, near_got, far_sent, far_got,
):
    my_donor = lax.axis_index("donor")
    my_var = lax.axis_index("var")
    don_rows = ct_ref.shape[1]
    cols = xv.shape[2]
    tiles = cols // TILE
    chunks = don_rows // TILE
    paths = members_ref.shape[1]
    genes_here = member_ref.shape[0]
    half = slab.shape[2]

    def donor_at(step):
        return lax.rem(my_donor + step, donors)

    def var_at(step):
        return lax.rem(my_var + step, groups)

    def load(turn):
        start = pl.multiple_of(donor_at(1 + turn) * cols, cols)
        return pltpu.make_async_copy(x_ref.at[:, pl.ds(start, cols)], xv.at[turn], x_sem.at[turn])

    for turn in range(donors):
        load(turn).start()

    barrier = pltpu.get_barrier_semaphore()
    for step in range(1, donors):
        pl.semaphore_signal(
            barrier, inc=1, device_id=(donor_at(step), my_var), device_id_type=MESH
        )

    def greet(step, carry):
        pl.semaphore_signal(
            barrier, inc=1, device_id=(my_donor, var_at(step)), device_id_type=MESH
        )
        return carry

    lax.fori_loop(1, groups, greet, 0)
    my_core = lax.rem(my_var, 2)
    my_chip = lax.div(my_var, 2)
    for step in range(1, donors):
        pl.semaphore_signal(
            barrier,
            inc=1,
            device_id=(donor_at(step), my_chip * 2 + 1 - my_core),
            device_id_type=MESH,
        )

    thrice = (iota((K, 256), 0) == lax.rem(iota((K, 256), 1), K)).astype(jnp.bfloat16)
    ct[0:K, :] = ct_ref[...]
    own = et_ref[...].astype(jnp.float32)
    ct[K:128, :] = jnp.concatenate(
        [own, jnp.zeros((128 - K - own.shape[0], don_rows), jnp.float32)], axis=0
    ).astype(jnp.bfloat16)
    small[my_donor] = lax.dot_general(
        ct[0:K, :], ct[...], (((1,), (1,)), ((), ())), preferred_element_type=jnp.float32
    )

    def prepare(chunk, carry):
        rows = pl.ds(pl.multiple_of(chunk * 512, 512), 512)
        ccc[rows, :] = lax.dot_general(
            ct[0:K, rows], thrice, (((0,), (0,)), ((), ())), preferred_element_type=jnp.float32
        ).astype(jnp.bfloat16)
        return carry

    lax.fori_loop(0, don_rows // 512, prepare, 0)
    slab[my_var] = jnp.concatenate([own[:, 0:half], own[:, half:]], axis=0).astype(jnp.bfloat16)

    def to_donor(step, src, dst, sent, got):
        return pltpu.make_async_remote_copy(
            src_ref=src,
            dst_ref=dst.at[my_donor],
            send_sem=sent.at[step],
            recv_sem=got.at[my_donor],
            device_id=(donor_at(step), my_var),
            device_id_type=MESH,
        )

    def from_donor(step, dst, sent, got):
        peer = donor_at(step)
        return pltpu.make_async_remote_copy(
            src_ref=dst.at[peer],
            dst_ref=dst.at[peer],
            send_sem=sent.at[step],
            recv_sem=got.at[peer],
            device_id=(peer, my_var),
            device_id_type=MESH,
        )


    def slab_copy(step):
        peer = var_at(step)
        return pltpu.make_async_remote_copy(
            src_ref=slab.at[my_var],
            dst_ref=slab.at[my_var],
            send_sem=slab_sent.at[step],
            recv_sem=slab_got.at[my_var],
            device_id=(my_donor, peer),
            device_id_type=MESH,
        )

    def slab_back(step):
        peer = var_at(step)
        return pltpu.make_async_remote_copy(
            src_ref=slab.at[peer],
            dst_ref=slab.at[peer],
            send_sem=slab_sent.at[step],
            recv_sem=slab_got.at[peer],
            device_id=(my_donor, peer),
            device_id_type=MESH,
        )

    def member_copy(step):
        peer = var_at(step)
        return pltpu.make_async_remote_copy(
            src_ref=member_ref.at[:, pl.ds(pl.multiple_of(peer * paths, 128), paths)],
            dst_ref=members_ref.at[pl.ds(pl.multiple_of(my_var * genes_here, 8), genes_here), :],
            send_sem=member_sent.at[step],
            recv_sem=member_got.at[my_var],
            device_id=(my_donor, peer),
            device_id_type=MESH,
        )

    def member_back(step):
        peer = var_at(step)
        rows = members_ref.at[pl.ds(pl.multiple_of(peer * genes_here, 8), genes_here), :]
        return pltpu.make_async_remote_copy(
            src_ref=rows,
            dst_ref=rows,
            send_sem=member_sent.at[step],
            recv_sem=member_got.at[peer],
            device_id=(my_donor, peer),
            device_id_type=MESH,
        )

    def each(first, last, act):
        def body(step, carry):
            act(step)
            return carry

        lax.fori_loop(first, last, body, 0)

    wide[...] = jnp.zeros_like(wide)
    shrink = lax.rsqrt(jnp.maximum(diagonal(small[my_donor]), 1e-30))

    sweeps = K // (2 * tiles)

    def moments(turn, mat):
        def body(tile, carry):
            if turn >= 2:
                for extra in range(sweeps):
                    carry = sweep(((turn - 2) * tiles + tile) * sweeps + extra, carry)
            lanes = pl.ds(pl.multiple_of(tile * TILE, TILE), TILE)
            product = jnp.dot(
                ct[0:K, :], xv[turn, :, lanes], preferred_element_type=jnp.float32
            )
            square = jnp.zeros((8, TILE), jnp.float32)
            for chunk in range(chunks):
                part = xv[turn, chunk * TILE : (chunk + 1) * TILE, lanes].astype(jnp.float32)
                square = square + jnp.sum((part * part).reshape(TILE // 8, 8, TILE), axis=0)
            rounded, step = steps_of(product * shrink)
            cross_out[turn, :, lanes] = rounded
            sides_out[turn, :, lanes] = two_rows(jnp.sum(square, axis=0, keepdims=True), step)
            return carry

        return lax.fori_loop(0, tiles, body, mat)

    mat = jnp.zeros((K, 128), jnp.float32)
    def send_cross(turn):
        step = turn + 1
        return (
            to_donor(step, cross_out.at[turn], cross_in, cross_sent, cross_got),
            to_donor(step, sides_out.at[turn], sides_in, sides_sent, sides_got),
        )

    for turn in range(donors):
        if turn == 2:
            for step in range(1, donors):
                from_donor(step, small, small_sent, small_got).wait_recv()
            for donor in range(donors):
                mat = mat + small[donor]
            mat = jnp.where(iota((K, 128), 1) < K, mat, 0.0)
            spread = jnp.maximum(diagonal(mat), 1e-30)
        load(turn).wait()
        mat = moments(turn, mat)
        if turn == 0:
            pl.semaphore_wait(barrier, 2 * donors + groups - 3)
            for step in range(1, donors):
                to_donor(step, small.at[my_donor], small, small_sent, small_got).start()
        if turn < donors - 1:
            for copy in send_cross(turn):
                copy.start()
        else:
            cross_in[my_donor] = cross_out[turn]
            sides_in[my_donor] = sides_out[turn]
        if turn == 0:
            each(1, groups, lambda step: slab_copy(step).start())
    inv_ref[...] = mat
    inverse = inv_ref[:, 0:K]

    each(1, groups, lambda step: member_copy(step).start())
    own_member = pltpu.make_async_copy(
        member_ref.at[:, pl.ds(pl.multiple_of(my_var * paths, 128), paths)],
        members_ref.at[pl.ds(pl.multiple_of(my_var * genes_here, 8), genes_here), :],
        own_sem,
    )
    own_member.start()


    for step in range(1, donors):
        from_donor(step, cross_in, cross_sent, cross_got).wait_recv()
        from_donor(step, sides_in, sides_sent, sides_got).wait_recv()
    sizes = [jnp.sqrt(jnp.maximum(diagonal(small[donor]), 1e-30)) for donor in range(donors)]
    widen, narrow = jnp.sqrt(spread), lax.rsqrt(spread)

    def solve(tile, carry):
        lanes = pl.ds(pl.multiple_of(tile * TILE, TILE), TILE)
        cross = jnp.zeros((K, TILE), jnp.float32)
        square = jnp.zeros((1, TILE), jnp.float32)
        for donor in range(donors):
            part = cross_in[donor, :, lanes].astype(jnp.int32).astype(jnp.float32)
            cross = cross + part * sides_in[donor, 1:2, lanes] * sizes[donor]
            square = square + sides_in[donor, 0:1, lanes]
        coef = jnp.dot(
            inverse, cross, precision=HIGHEST, preferred_element_type=jnp.float32
        )
        left = square - jnp.sum(cross * coef, axis=0, keepdims=True)
        scale = lax.rsqrt(jnp.maximum(left, 0.0) + EPSILON)
        rounded, step = steps_of(coef * scale * widen)
        beta[my_donor, :, lanes] = rounded
        beta_sides[my_donor, :, lanes] = two_rows(scale, step)
        return carry

    lax.fori_loop(0, tiles, solve, 0)

    def send_beta(step):
        return (
            to_donor(step, beta.at[my_donor], beta, beta_sent, beta_got),
            to_donor(step, beta_sides.at[my_donor], beta_sides, scale_sent, scale_got),
        )

    for step in range(1, donors):
        for copy in send_beta(step):
            copy.start()

    each(1, groups, lambda step: slab_back(step).wait_recv())
    per_copy = 4

    def unfold(index, carry):
        first = pl.multiple_of(index * per_copy, per_copy)
        part = slab[pl.ds(first, per_copy)].astype(jnp.float32)
        rows = pl.ds(pl.multiple_of(first * 8, per_copy * 8), per_copy * 8)
        expr_t[rows, 0:half] = part[:, 0:8, :].reshape(per_copy * 8, half).astype(jnp.bfloat16)
        expr_t[rows, half : 2 * half] = (
            part[:, 8:16, :].reshape(per_copy * 8, half).astype(jnp.bfloat16)
        )
        return carry

    lax.fori_loop(0, groups // per_copy, unfold, 0)

    genes_all = expr_t.shape[0]
    expr_sums[my_donor, 0:K, :] = lax.dot_general(
        ct[0:K, :], expr_t[...], (((1,), (1,)), ((), ())), preferred_element_type=jnp.float32
    )
    square = jnp.zeros((genes_all, 128), jnp.float32)
    for first in range(0, don_rows, 128):
        part = expr_t[:, first : first + 128].astype(jnp.float32)
        square = square + part * part
    expr_sums[my_donor, K:ROWS, :] = lax.dot_general(
        jnp.ones((ROWS - K, 128), jnp.float32),
        square,
        (((1,), (1,)), ((), ())),
        precision=HIGHEST,
        preferred_element_type=jnp.float32,
    )
    for step in range(1, donors):
        to_donor(step, expr_sums.at[my_donor], expr_sums, expr_sent, expr_got).start()

    def turn_of(step):
        return (step + donors - 1) % donors

    def standardize(step, tile):
        owner, turn = donor_at(step), turn_of(step)
        lanes = pl.ds(pl.multiple_of(tile * TILE, TILE), TILE)
        coef = beta[owner, :, lanes].astype(jnp.int32).astype(jnp.float32)
        coef = coef * beta_sides[owner, 1:2, lanes] * narrow
        scale = beta_sides[owner, 0:1, lanes]
        for piece in range(3):
            rounded = coef.astype(jnp.bfloat16)
            pieces[piece * K : (piece + 1) * K, :] = rounded
            coef = coef - rounded.astype(jnp.float32)
        for first in range(0, don_rows, STRIP):
            rows = slice(first, first + STRIP)
            fitted = jnp.dot(ccc[rows, 0 : 3 * K], pieces[...], preferred_element_type=jnp.float32)
            part = xv[turn, rows, lanes].astype(jnp.float32)
            xv[turn, rows, lanes] = (part * scale - fitted).astype(jnp.bfloat16)

    def pick(step, tile):
        owner, turn = donor_at(step), turn_of(step)
        lanes = pl.ds(pl.multiple_of(tile * TILE, TILE), TILE)
        found = jnp.dot(expr_t[...], xv[turn, :, lanes], preferred_element_type=jnp.float32)
        for side in range(TILE // VB):
            wide[side, PAD : PAD + genes_all, :] = found[:, side * VB : (side + 1) * VB]
        for side in range(TILE // VB):
            block = tile * (TILE // VB) + side
            place = place_ref[owner * (cols // VB) + block]
            base = jnp.right_shift(place - LEAD, 2) + PAD
            found = wide[side, pl.ds(base, 16), :]
            if step:
                slot_out[step, block] = found
            else:
                slot_in[my_donor, block] = found

    each(0, tiles, lambda tile: standardize(0, tile))

    for step in range(1, donors):
        from_donor(step, expr_sums, expr_sent, expr_got).wait_recv()
    sums = expr_sums[0]
    for donor in range(1, donors):
        sums = sums + expr_sums[donor]
    sums = jnp.concatenate([sums, jnp.zeros((128 - ROWS, genes_all), jnp.float32)], axis=0)
    sums = jnp.transpose(sums)
    expr_coef = jnp.dot(
        sums[:, 0:K], inv_ref[...], precision=HIGHEST, preferred_element_type=jnp.float32
    )
    in_cov = iota((genes_all, 128), 1) < K
    expr_ss = sums[:, K : K + 1] - jnp.sum(
        jnp.where(in_cov, sums * expr_coef, 0.0), axis=1, keepdims=True
    )
    expr_scale = lax.rsqrt(jnp.maximum(expr_ss, 0.0) + EPSILON)
    expr_pieces = []
    for piece in range(3):
        rounded = expr_coef.astype(jnp.bfloat16)
        expr_pieces.append(rounded)
        expr_coef = expr_coef - rounded.astype(jnp.float32)
    for first in range(0, don_rows, STRIP):
        lanes = slice(first, first + STRIP)
        resid = expr_t[:, lanes].astype(jnp.float32)
        for part in expr_pieces:
            resid = resid - jnp.dot(part, ct[:, lanes], preferred_element_type=jnp.float32)
        expr_t[:, lanes] = (resid * expr_scale).astype(jnp.bfloat16)

    each(0, tiles, lambda tile: pick(0, tile))
    for step in (1, 3, 2):
        from_donor(step, beta, beta_sent, beta_got).wait_recv()
        from_donor(step, beta_sides, scale_sent, scale_got).wait_recv()

        def both(tile, step=step):
            standardize(step, tile)
            pick(step, tile)

        each(0, tiles, both)
        to_donor(step, slot_out.at[step], slot_in, slot_sent, slot_got).start()

    for step in range(1, donors):
        from_donor(step, slot_in, slot_sent, slot_got).wait_recv()
    donors_all = don_rows * donors
    starts, counts = start_ref[...], count_ref[...]
    gene_row = iota((16, genes_all), 1)
    slot_row = iota((16, genes_all), 0)
    gene_part = jnp.zeros((1, genes_all), jnp.float32)
    for block in range(slot_in.shape[1]):
        total = slot_in[0, block]
        for donor in range(1, donors):
            total = total + slot_in[donor, block]
        terms = jnp.sum(
            cauchy_terms(total * math.sqrt(donors_all - K - 2)), axis=1, keepdims=True
        )
        place = place_ref[my_donor * slot_in.shape[1] + block]
        base = jnp.right_shift(place - LEAD, 2)
        live = (starts <= place) & (place < starts + counts)
        here = (gene_row == slot_row + base) & (slot_row < GMAX)
        column = jnp.sum(jnp.where(here, terms, 0.0), axis=0, keepdims=True)
        gene_part = gene_part + jnp.where(live, column, 0.0)

    near_count, far_count = donors * 2, groups // 2
    my_near = my_donor * 2 + my_core

    def near_id(step):
        place = lax.rem(my_near + step, near_count)
        return place, (lax.div(place, 2), my_chip * 2 + lax.rem(place, 2))

    def far_id(step):
        place = lax.rem(my_chip + step, far_count)
        return place, (my_donor, place * 2 + my_core)

    tail = []
    for buffer, mine, count, where, sent, got in (
        (near, my_near, near_count, near_id, near_sent, near_got),
        (far, my_chip, far_count, far_id, far_sent, far_got),
    ):
        buffer[mine] = gene_part
        for step in range(1, count):
            copy = pltpu.make_async_remote_copy(
                src_ref=buffer.at[mine],
                dst_ref=buffer.at[mine],
                send_sem=sent.at[step],
                recv_sem=got.at[mine],
                device_id=where(step)[1],
                device_id_type=MESH,
            )
            copy.start()
            tail.append(copy)
        for step in range(1, count):
            peer, device = where(step)
            pltpu.make_async_remote_copy(
                src_ref=buffer.at[peer],
                dst_ref=buffer.at[peer],
                send_sem=sent.at[step],
                recv_sem=got.at[peer],
                device_id=device,
                device_id_type=MESH,
            ).wait_recv()
        gene_part = buffer[0]
        for index in range(1, count):
            gene_part = gene_part + buffer[index]

    covered = jnp.minimum(starts + counts, total_blocks) - jnp.maximum(starts, 0)
    gene_stat = gene_part / (VB * covered).astype(jnp.float32)
    gene_value = 0.5 - arctan(gene_stat) / math.pi
    own_gene = iota((genes_here, genes_all), 1) == iota((genes_here, genes_all), 0) + my_var * genes_here
    gene_ref[...] = jnp.broadcast_to(
        jnp.sum(jnp.where(own_gene, gene_value, 0.0), axis=1, keepdims=True), gene_ref.shape
    )
    own_member.wait()
    each(1, groups, lambda step: member_back(step).wait_recv())
    members = members_ref[...]
    path_sum = jnp.dot(
        jnp.broadcast_to(gene_stat, (8, genes_all)),
        members,
        precision=HIGHEST,
        preferred_element_type=jnp.float32,
    )
    path_weight = jnp.sum(members, axis=0, keepdims=True)
    path_ref[...] = (
        0.5 - arctan(path_sum[0:1, :] / jnp.maximum(path_weight, 1.0)) / math.pi
    )
    each(1, groups, lambda step: member_copy(step).wait_send())
    each(1, groups, lambda step: slab_copy(step).wait_send())
    for step in range(1, donors):
        to_donor(step, small.at[my_donor], small, small_sent, small_got).wait_send()
        for copy in (*send_cross(step - 1), *send_beta(step)):
            copy.wait_send()
        to_donor(step, expr_sums.at[my_donor], expr_sums, expr_sent, expr_got).wait_send()
        to_donor(step, slot_out.at[step], slot_in, slot_sent, slot_got).wait_send()
    for copy in tail:
        copy.wait_send()


def local(genotype, block_place, expression, covariates, gene_start, gene_count, membership):
    don_rows, var_cols = genotype.shape
    blocks_here = block_place.shape[0]
    genes_all = gene_start.shape[0]
    genes_here = expression.shape[1]
    groups = lax.axis_size("var")
    donors = lax.axis_size("donor")
    total_blocks = blocks_here * groups
    paths_here = membership.shape[1] // groups
    cols = var_cols // donors
    blocks_own = blocks_here // donors

    vmem = pl.BlockSpec(memory_space=pltpu.VMEM)
    anywhere = pl.BlockSpec(memory_space=pl.ANY)
    dma = pltpu.SemaphoreType.DMA

    def body(*refs):
        correlate(donors, groups, total_blocks, *refs)

    gene_value, path_value = pl.pallas_call(
        body,
        out_shape=(
            jax.ShapeDtypeStruct((genes_here, 128), jnp.float32),
            jax.ShapeDtypeStruct((1, paths_here), jnp.float32),
        ),
        in_specs=[vmem, vmem, pl.BlockSpec(memory_space=pltpu.SMEM), vmem, vmem, anywhere, anywhere],
        out_specs=(vmem, vmem),
        scratch_shapes=[
            pltpu.VMEM((genes_all, paths_here), jnp.float32),
            pltpu.VMEM((donors, don_rows, cols), jnp.bfloat16),
            pltpu.VMEM((128, don_rows), jnp.bfloat16),
            pltpu.VMEM((don_rows, 256), jnp.bfloat16),
            pltpu.VMEM((donors, K, 128), jnp.float32),
            pltpu.VMEM((K, 128), jnp.float32),
            pltpu.VMEM((donors, K, cols), jnp.int16),
            pltpu.VMEM((donors, 8, cols), jnp.float32),
            pltpu.VMEM((donors, K, cols), jnp.int16),
            pltpu.VMEM((donors, 8, cols), jnp.float32),
            pltpu.VMEM((donors, K, cols), jnp.int16),
            pltpu.VMEM((donors, 8, cols), jnp.float32),
            pltpu.VMEM((groups, 16, don_rows // 2), jnp.bfloat16),
            pltpu.VMEM((genes_all, don_rows), jnp.bfloat16),
            pltpu.VMEM((donors, ROWS, genes_all), jnp.float32),
            pltpu.VMEM((3 * K, TILE), jnp.bfloat16),
            pltpu.VMEM((TILE // VB, genes_all + 24, VB), jnp.float32),
            pltpu.VMEM((donors, blocks_own, 16, VB), jnp.float32),
            pltpu.VMEM((donors, blocks_own, 16, VB), jnp.float32),
            pltpu.VMEM((donors * 2, 1, genes_all), jnp.float32),
            pltpu.VMEM((groups // 2, 1, genes_all), jnp.float32),
            *[dma((donors,)) for _ in range(15)],
            *[dma((groups,)) for _ in range(4)],
            dma,
            *[dma((donors * 2,)) for _ in range(2)],
            *[dma((groups // 2,)) for _ in range(2)],
        ],
        compiler_params=pltpu.CompilerParams(
            collective_id=0, has_side_effects=True, vmem_limit_bytes=56 * 2**20
        ),
        name="correlate",
    )(
        covariates.T,
        expression.T,
        block_place,
        gene_start.reshape(1, genes_all),
        gene_count.reshape(1, genes_all),
        genotype,
        membership,
    )

    return (gene_value[:, 0], path_value[0])


def solution(mesh):
    placed = (
        P("donor", "var"),
        P("var"),
        P("donor", "var"),
        P("donor", None),
        P(),
        P(),
        P("var", None),
    )
    return jax.shard_map(
        local, mesh=mesh, in_specs=placed, out_specs=(P("var"), P("var")), check_vma=False
    )
```

time: 129 us -> 73.4 us (0.57)
  Pallas kernels: 118 us -> 70 us
  other arithmetic: 6.4 us -> 1.26 us
  matrix products: 1.31 us -> 0 us
    pallas_call x2 -> x1, Pallas kernels: 118 us -> 70 us  [local(): pl.pallas_call(body, out_shape=(jax.ShapeDtypeStruct((genes_here, 128), j...]
    reduce_sum x3 -> x0, other arithmetic: 3.03 us -> none  [the longest x1 1.31 us: local(): jnp.sum(cauchy_terms(corr * math.sqrt(donors_all - K - 2)), axis=2)]
    unnamed x8 -> x0, local copies, waits for them, and re-layouts: 2.41 us -> none
    dot_general x1 -> x0, matrix products: 1.31 us -> none  [local(): path_sum = jnp.dot(gene_stat, members, precision=HIGHEST)]
    slice x0 -> x1, local copies, waits for them, and re-layouts: none -> 1.31 us  [local(): return (gene_value[:, 0], path_value[0])]
where the time goes in v2:
time: 73.4 us; the launch traced here: 73.2 us
  Pallas kernels  70 us (95%)
  local copies, waits for them, and re-layouts  1.31 us (2%)
  other arithmetic  1.26 us (2%)
    pallas_call x1, Pallas kernels, local(): pl.pallas_call(body, out_shape=(jax.ShapeDtypeStruct((genes_here, 128), j...  70 us

profile of v2, /device:TPU:1, one launch (start us, length us, event | category | flops | bytes accessed | tf_op | source)
XLA Modules:
  0.0 73.2 jit_solution(12336623348537122537)
XLA Ops:
  0.6 70.0 %correlate.1 = (f32[8,128]{1,0:T(8,128)}, f32[1,384]{1,0:T(1,128)}) custom-call(bf16[64,2560]{1,0:T(8,128)(2,1)} %bitcast.4, bf16[8,2560]{1,0:T(8,128)(2,1)} %bitcast.5, s32[32]{0:T(128)} %refs_2_.1, s32[1,256]{1,0:T(1,128)} %bitcast.6, s32[1,256]{1,0:T(1,128)} %bitcast.7, bf16[2560,4096]{1,0:T(8,128)(2,1)} %refs_5_.1, f32[8,12288]{1,0:T(8,128)} %refs_6_.1), custom_call_target="tpu_custom_call" | custom-call | tf_op jit(solution)/shard_map/correlate/pallas_call | solution.py:573
  70.6 1.3 %slice_reduce_fusion = f32[8]{0:T(128)} fusion(f32[8,128]{1,0:T(8,128)} %get-tuple-element.4), kind=kLoop, calls=%fused_computation | loop fusion | bytes 64 | tf_op jit(solution)/shard_map/slice | solution.py:623
  71.9 1.3 %reduce.1 = f32[384]{0:T(512)} reduce(f32[1,384]{1,0:T(1,128)} %get-tuple-element.5, f32[]{:T(128)} %constant.2), dimensions={0}, to_apply=%get-tuple-element.5.reduce_sub_computation | reduce | bytes 3076 | tf_op jit(solution)/shard_map/correlate/pallas_call | solution.py:573

commit v3 on v2

--- a/solution.py
+++ b/solution.py
@@ -101,8 +101,8 @@
     donors, groups, total_blocks, ct_ref, et_ref, place_ref, start_ref, count_ref, x_ref, member_ref, gene_ref, path_ref,
     members_ref, xv, ct, ccc, small, inv_ref, cross_out, sides_out, cross_in, sides_in, beta, beta_sides, slab, expr_t, expr_sums, pieces, wide,
     slot_out, slot_in, near, far,
-    x_sem, small_sent, small_got, cross_sent, cross_got, sides_sent, sides_got, beta_sent, beta_got, scale_sent, scale_got, expr_sent, expr_got, slot_sent, slot_got,
-    slab_sent, slab_got, member_sent, member_got, own_sem, near_sent, near_got, far_sent, far_got,
+    x_sem, small_sent, small_got, cross_sent, cross_got, sides_sent, sides_got, beta_sent, beta_got, scale_sent, scale_got, slot_sent, slot_got,
+    slab_sent, slab_got, expr_sent, expr_got, member_sent, member_got, own_sem, near_sent, near_got, far_sent, far_got,
 ):
     my_donor = lax.axis_index("donor")
     my_var = lax.axis_index("var")
@@ -157,8 +157,8 @@
         [own, jnp.zeros((128 - K - own.shape[0], don_rows), jnp.float32)], axis=0
     ).astype(jnp.bfloat16)
     small[my_donor] = lax.dot_general(
-        ct[0:K, :], ct[...], (((1,), (1,)), ((), ())), preferred_element_type=jnp.float32
-    )
+        ct[...], ct[...], (((1,), (1,)), ((), ())), preferred_element_type=jnp.float32
+    )[0:ROWS, :]
 
     def prepare(chunk, carry):
         rows = pl.ds(pl.multiple_of(chunk * 512, 512), 512)
@@ -245,7 +245,7 @@
         lax.fori_loop(first, last, body, 0)
 
     wide[...] = jnp.zeros_like(wide)
-    shrink = lax.rsqrt(jnp.maximum(diagonal(small[my_donor]), 1e-30))
+    shrink = lax.rsqrt(jnp.maximum(diagonal(small[my_donor, 0:K, :]), 1e-30))
 
     sweeps = K // (2 * tiles)
 
@@ -281,8 +281,10 @@
         if turn == 2:
             for step in range(1, donors):
                 from_donor(step, small, small_sent, small_got).wait_recv()
+            expr_rows = jnp.zeros((ROWS - K, 128), jnp.float32)
             for donor in range(donors):
-                mat = mat + small[donor]
+                mat = mat + small[donor, 0:K, :]
+                expr_rows = expr_rows + small[donor, K:ROWS, :]
             mat = jnp.where(iota((K, 128), 1) < K, mat, 0.0)
             spread = jnp.maximum(diagonal(mat), 1e-30)
         load(turn).wait()
@@ -302,6 +304,42 @@
     inv_ref[...] = mat
     inverse = inv_ref[:, 0:K]
 
+    coef_shape = (genes_here, 128)
+    expr_coef = jnp.dot(
+        expr_rows[:, 0:K], mat, precision=HIGHEST, preferred_element_type=jnp.float32
+    )
+    on_own = iota(coef_shape, 1) == iota(coef_shape, 0) + K
+    expr_sq = jnp.sum(jnp.where(on_own, expr_rows, 0.0), axis=1, keepdims=True)
+    in_cov = iota(coef_shape, 1) < K
+    expr_ss = expr_sq - jnp.sum(
+        jnp.where(in_cov, expr_rows * expr_coef, 0.0), axis=1, keepdims=True
+    )
+    expr_scale = lax.rsqrt(jnp.maximum(expr_ss, 0.0) + EPSILON)
+    expr_sums[my_var] = jnp.where(in_cov, expr_coef, expr_scale)
+
+    def coef_copy(step):
+        return pltpu.make_async_remote_copy(
+            src_ref=expr_sums.at[my_var],
+            dst_ref=expr_sums.at[my_var],
+            send_sem=expr_sent.at[step],
+            recv_sem=expr_got.at[my_var],
+            device_id=(my_donor, var_at(step)),
+            device_id_type=MESH,
+        )
+
+    def coef_back(step):
+        peer = var_at(step)
+        return pltpu.make_async_remote_copy(
+            src_ref=expr_sums.at[peer],
+            dst_ref=expr_sums.at[peer],
+            send_sem=expr_sent.at[step],
+            recv_sem=expr_got.at[peer],
+            device_id=(my_donor, peer),
+            device_id_type=MESH,
+        )
+
+    each(1, groups, lambda step: coef_copy(step).start())
+
     each(1, groups, lambda step: member_copy(step).start())
     own_member = pltpu.make_async_copy(
         member_ref.at[:, pl.ds(pl.multiple_of(my_var * paths, 128), paths)],
@@ -314,7 +352,7 @@
     for step in range(1, donors):
         from_donor(step, cross_in, cross_sent, cross_got).wait_recv()
         from_donor(step, sides_in, sides_sent, sides_got).wait_recv()
-    sizes = [jnp.sqrt(jnp.maximum(diagonal(small[donor]), 1e-30)) for donor in range(donors)]
+    sizes = [jnp.sqrt(jnp.maximum(diagonal(small[donor, 0:K, :]), 1e-30)) for donor in range(donors)]
     widen, narrow = jnp.sqrt(spread), lax.rsqrt(spread)
 
     def solve(tile, carry):
@@ -343,42 +381,11 @@
             to_donor(step, beta_sides.at[my_donor], beta_sides, scale_sent, scale_got),
         )
 
-    for step in range(1, donors):
+    for step in (1, 3, 2):
         for copy in send_beta(step):
             copy.start()
 
-    each(1, groups, lambda step: slab_back(step).wait_recv())
-    per_copy = 4
-
-    def unfold(index, carry):
-        first = pl.multiple_of(index * per_copy, per_copy)
-        part = slab[pl.ds(first, per_copy)].astype(jnp.float32)
-        rows = pl.ds(pl.multiple_of(first * 8, per_copy * 8), per_copy * 8)
-        expr_t[rows, 0:half] = part[:, 0:8, :].reshape(per_copy * 8, half).astype(jnp.bfloat16)
-        expr_t[rows, half : 2 * half] = (
-            part[:, 8:16, :].reshape(per_copy * 8, half).astype(jnp.bfloat16)
-        )
-        return carry
-
-    lax.fori_loop(0, groups // per_copy, unfold, 0)
-
     genes_all = expr_t.shape[0]
-    expr_sums[my_donor, 0:K, :] = lax.dot_general(
-        ct[0:K, :], expr_t[...], (((1,), (1,)), ((), ())), preferred_element_type=jnp.float32
-    )
-    square = jnp.zeros((genes_all, 128), jnp.float32)
-    for first in range(0, don_rows, 128):
-        part = expr_t[:, first : first + 128].astype(jnp.float32)
-        square = square + part * part
-    expr_sums[my_donor, K:ROWS, :] = lax.dot_general(
-        jnp.ones((ROWS - K, 128), jnp.float32),
-        square,
-        (((1,), (1,)), ((), ())),
-        precision=HIGHEST,
-        preferred_element_type=jnp.float32,
-    )
-    for step in range(1, donors):
-        to_donor(step, expr_sums.at[my_donor], expr_sums, expr_sent, expr_got).start()
 
     def turn_of(step):
         return (step + donors - 1) % donors
@@ -417,21 +424,24 @@
 
     each(0, tiles, lambda tile: standardize(0, tile))
 
-    for step in range(1, donors):
-        from_donor(step, expr_sums, expr_sent, expr_got).wait_recv()
-    sums = expr_sums[0]
-    for donor in range(1, donors):
-        sums = sums + expr_sums[donor]
-    sums = jnp.concatenate([sums, jnp.zeros((128 - ROWS, genes_all), jnp.float32)], axis=0)
-    sums = jnp.transpose(sums)
-    expr_coef = jnp.dot(
-        sums[:, 0:K], inv_ref[...], precision=HIGHEST, preferred_element_type=jnp.float32
-    )
-    in_cov = iota((genes_all, 128), 1) < K
-    expr_ss = sums[:, K : K + 1] - jnp.sum(
-        jnp.where(in_cov, sums * expr_coef, 0.0), axis=1, keepdims=True
-    )
-    expr_scale = lax.rsqrt(jnp.maximum(expr_ss, 0.0) + EPSILON)
+    each(1, groups, lambda step: slab_back(step).wait_recv())
+    per_copy = 4
+
+    def unfold(index, carry):
+        first = pl.multiple_of(index * per_copy, per_copy)
+        part = slab[pl.ds(first, per_copy)].astype(jnp.float32)
+        rows = pl.ds(pl.multiple_of(first * 8, per_copy * 8), per_copy * 8)
+        expr_t[rows, 0:half] = part[:, 0:8, :].reshape(per_copy * 8, half).astype(jnp.bfloat16)
+        expr_t[rows, half : 2 * half] = (
+            part[:, 8:16, :].reshape(per_copy * 8, half).astype(jnp.bfloat16)
+        )
+        return carry
+
+    lax.fori_loop(0, groups // per_copy, unfold, 0)
+    each(1, groups, lambda step: coef_back(step).wait_recv())
+    expr_coef = expr_sums[...].reshape(genes_all, 128)
+    expr_scale = expr_coef[:, K : K + 1]
+    expr_coef = jnp.where(iota((genes_all, 128), 1) < K, expr_coef, 0.0)
     expr_pieces = []
     for piece in range(3):
         rounded = expr_coef.astype(jnp.bfloat16)
@@ -541,11 +551,11 @@
     )
     each(1, groups, lambda step: member_copy(step).wait_send())
     each(1, groups, lambda step: slab_copy(step).wait_send())
+    each(1, groups, lambda step: coef_copy(step).wait_send())
     for step in range(1, donors):
         to_donor(step, small.at[my_donor], small, small_sent, small_got).wait_send()
         for copy in (*send_cross(step - 1), *send_beta(step)):
             copy.wait_send()
-        to_donor(step, expr_sums.at[my_donor], expr_sums, expr_sent, expr_got).wait_send()
         to_donor(step, slot_out.at[step], slot_in, slot_sent, slot_got).wait_send()
     for copy in tail:
         copy.wait_send()
@@ -583,7 +593,7 @@
             pltpu.VMEM((donors, don_rows, cols), jnp.bfloat16),
             pltpu.VMEM((128, don_rows), jnp.bfloat16),
             pltpu.VMEM((don_rows, 256), jnp.bfloat16),
-            pltpu.VMEM((donors, K, 128), jnp.float32),
+            pltpu.VMEM((donors, ROWS, 128), jnp.float32),
             pltpu.VMEM((K, 128), jnp.float32),
             pltpu.VMEM((donors, K, cols), jnp.int16),
             pltpu.VMEM((donors, 8, cols), jnp.float32),
@@ -593,15 +603,15 @@
             pltpu.VMEM((donors, 8, cols), jnp.float32),
             pltpu.VMEM((groups, 16, don_rows // 2), jnp.bfloat16),
             pltpu.VMEM((genes_all, don_rows), jnp.bfloat16),
-            pltpu.VMEM((donors, ROWS, genes_all), jnp.float32),
+            pltpu.VMEM((groups, genes_here, 128), jnp.float32),
             pltpu.VMEM((3 * K, TILE), jnp.bfloat16),
             pltpu.VMEM((TILE // VB, genes_all + 24, VB), jnp.float32),
             pltpu.VMEM((donors, blocks_own, 16, VB), jnp.float32),
             pltpu.VMEM((donors, blocks_own, 16, VB), jnp.float32),
             pltpu.VMEM((donors * 2, 1, genes_all), jnp.float32),
             pltpu.VMEM((groups // 2, 1, genes_all), jnp.float32),
-            *[dma((donors,)) for _ in range(15)],
-            *[dma((groups,)) for _ in range(4)],
+            *[dma((donors,)) for _ in range(13)],
+            *[dma((groups,)) for _ in range(6)],
             dma,
             *[dma((donors * 2,)) for _ in range(2)],
             *[dma((groups // 2,)) for _ in range(2)],

time: 73.4 us -> 69.6 us (0.948)
  Pallas kernels: 70 us -> 66.2 us
    pallas_call x1, Pallas kernels: 70 us -> 66.2 us  [local(): pl.pallas_call(body, out_shape=(jax.ShapeDtypeStruct((genes_here, 128), j...]
where the time goes in v3:
time: 69.6 us; the launch traced here: 69.4 us
  Pallas kernels  66.2 us (95%)
  local copies, waits for them, and re-layouts  1.31 us (2%)
  other arithmetic  1.26 us (2%)
    pallas_call x1, Pallas kernels, local(): pl.pallas_call(body, out_shape=(jax.ShapeDtypeStruct((genes_here, 128), j...  66.2 us

profile of v3, /device:TPU:1, one launch (start us, length us, event | category | flops | bytes accessed | tf_op | source)
XLA Modules:
  0.0 69.4 jit_solution(2871986862244710605)
XLA Ops:
  0.6 66.2 %correlate.1 = (f32[8,128]{1,0:T(8,128)}, f32[1,384]{1,0:T(1,128)}) custom-call(bf16[64,2560]{1,0:T(8,128)(2,1)} %bitcast.4, bf16[8,2560]{1,0:T(8,128)(2,1)} %bitcast.5, s32[32]{0:T(128)} %refs_2_.1, s32[1,256]{1,0:T(1,128)} %bitcast.6, s32[1,256]{1,0:T(1,128)} %bitcast.7, bf16[2560,4096]{1,0:T(8,128)(2,1)} %refs_5_.1, f32[8,12288]{1,0:T(8,128)} %refs_6_.1), custom_call_target="tpu_custom_call" | custom-call | tf_op jit(solution)/shard_map/correlate/pallas_call | solution.py:583
  66.9 1.3 %slice_reduce_fusion = f32[8]{0:T(128)} fusion(f32[8,128]{1,0:T(8,128)} %get-tuple-element.4), kind=kLoop, calls=%fused_computation | loop fusion | bytes 64 | tf_op jit(solution)/shard_map/slice | solution.py:633
  68.2 1.3 %reduce.1 = f32[384]{0:T(512)} reduce(f32[1,384]{1,0:T(1,128)} %get-tuple-element.5, f32[]{:T(128)} %constant.2), dimensions={0}, to_apply=%get-tuple-element.5.reduce_sub_computation | reduce | bytes 3076 | tf_op jit(solution)/shard_map/correlate/pallas_call | solution.py:583

commit v4 on v3

--- a/solution.py
+++ b/solution.py
@@ -390,33 +390,41 @@
     def turn_of(step):
         return (step + donors - 1) % donors
 
+    def lanes_of(tile):
+        if isinstance(tile, int):
+            return slice(tile * TILE, (tile + 1) * TILE)
+        return pl.ds(pl.multiple_of(tile * TILE, TILE), TILE)
+
+    def spot(tile):
+        return tile % 2 if isinstance(tile, int) else 0
+
     def standardize(step, tile):
         owner, turn = donor_at(step), turn_of(step)
-        lanes = pl.ds(pl.multiple_of(tile * TILE, TILE), TILE)
+        lanes = lanes_of(tile)
         coef = beta[owner, :, lanes].astype(jnp.int32).astype(jnp.float32)
         coef = coef * beta_sides[owner, 1:2, lanes] * narrow
         scale = beta_sides[owner, 0:1, lanes]
         for piece in range(3):
             rounded = coef.astype(jnp.bfloat16)
-            pieces[piece * K : (piece + 1) * K, :] = rounded
+            pieces[spot(tile), piece * K : (piece + 1) * K, :] = rounded
             coef = coef - rounded.astype(jnp.float32)
         for first in range(0, don_rows, STRIP):
             rows = slice(first, first + STRIP)
-            fitted = jnp.dot(ccc[rows, 0 : 3 * K], pieces[...], preferred_element_type=jnp.float32)
+            fitted = jnp.dot(ccc[rows, 0 : 3 * K], pieces[spot(tile)], preferred_element_type=jnp.float32)
             part = xv[turn, rows, lanes].astype(jnp.float32)
             xv[turn, rows, lanes] = (part * scale - fitted).astype(jnp.bfloat16)
 
     def pick(step, tile):
         owner, turn = donor_at(step), turn_of(step)
-        lanes = pl.ds(pl.multiple_of(tile * TILE, TILE), TILE)
+        lanes = lanes_of(tile)
         found = jnp.dot(expr_t[...], xv[turn, :, lanes], preferred_element_type=jnp.float32)
         for side in range(TILE // VB):
-            wide[side, PAD : PAD + genes_all, :] = found[:, side * VB : (side + 1) * VB]
+            wide[2 * spot(tile) + side, PAD : PAD + genes_all, :] = found[:, side * VB : (side + 1) * VB]
         for side in range(TILE // VB):
             block = tile * (TILE // VB) + side
             place = place_ref[owner * (cols // VB) + block]
             base = jnp.right_shift(place - LEAD, 2) + PAD
-            found = wide[side, pl.ds(base, 16), :]
+            found = wide[2 * spot(tile) + side, pl.ds(base, 16), :]
             if step:
                 slot_out[step, block] = found
             else:
@@ -459,11 +467,11 @@
         from_donor(step, beta, beta_sent, beta_got).wait_recv()
         from_donor(step, beta_sides, scale_sent, scale_got).wait_recv()
 
-        def both(tile, step=step):
-            standardize(step, tile)
+        standardize(step, 0)
+        for tile in range(tiles):
+            if tile + 1 < tiles:
+                standardize(step, tile + 1)
             pick(step, tile)
-
-        each(0, tiles, both)
         to_donor(step, slot_out.at[step], slot_in, slot_sent, slot_got).start()
 
     for step in range(1, donors):
@@ -604,8 +612,8 @@
             pltpu.VMEM((groups, 16, don_rows // 2), jnp.bfloat16),
             pltpu.VMEM((genes_all, don_rows), jnp.bfloat16),
             pltpu.VMEM((groups, genes_here, 128), jnp.float32),
-            pltpu.VMEM((3 * K, TILE), jnp.bfloat16),
-            pltpu.VMEM((TILE // VB, genes_all + 24, VB), jnp.float32),
+            pltpu.VMEM((2, 3 * K, TILE), jnp.bfloat16),
+            pltpu.VMEM((2 * (TILE // VB), genes_all + 24, VB), jnp.float32),
             pltpu.VMEM((donors, blocks_own, 16, VB), jnp.float32),
             pltpu.VMEM((donors, blocks_own, 16, VB), jnp.float32),
             pltpu.VMEM((donors * 2, 1, genes_all), jnp.float32),

time: 69.6 us -> 66.2 us (0.951)
  Pallas kernels: 66.2 us -> 62.8 us
    pallas_call x1, Pallas kernels: 66.2 us -> 62.8 us  [local(): pl.pallas_call(body, out_shape=(jax.ShapeDtypeStruct((genes_here, 128), j...]
where the time goes in v4:
time: 66.2 us; the launch traced here: 66 us
  Pallas kernels  62.8 us (95%)
  local copies, waits for them, and re-layouts  1.31 us (2%)
  other arithmetic  1.26 us (2%)
    pallas_call x1, Pallas kernels, local(): pl.pallas_call(body, out_shape=(jax.ShapeDtypeStruct((genes_here, 128), j...  62.8 us

profile of v4, /device:TPU:1, one launch (start us, length us, event | category | flops | bytes accessed | tf_op | source)
XLA Modules:
  0.0 66.0 jit_solution(5368256675513481063)
XLA Ops:
  0.6 62.8 %correlate.1 = (f32[8,128]{1,0:T(8,128)}, f32[1,384]{1,0:T(1,128)}) custom-call(bf16[64,2560]{1,0:T(8,128)(2,1)} %bitcast.4, bf16[8,2560]{1,0:T(8,128)(2,1)} %bitcast.5, s32[32]{0:T(128)} %refs_2_.1, s32[1,256]{1,0:T(1,128)} %bitcast.6, s32[1,256]{1,0:T(1,128)} %bitcast.7, bf16[2560,4096]{1,0:T(8,128)(2,1)} %refs_5_.1, f32[8,12288]{1,0:T(8,128)} %refs_6_.1), custom_call_target="tpu_custom_call" | custom-call | tf_op jit(solution)/shard_map/correlate/pallas_call | solution.py:591
  63.5 1.3 %slice_reduce_fusion = f32[8]{0:T(128)} fusion(f32[8,128]{1,0:T(8,128)} %get-tuple-element.4), kind=kLoop, calls=%fused_computation | loop fusion | bytes 64 | tf_op jit(solution)/shard_map/slice | solution.py:641
  64.8 1.3 %reduce.1 = f32[384]{0:T(512)} reduce(f32[1,384]{1,0:T(1,128)} %get-tuple-element.5, f32[]{:T(128)} %constant.2), dimensions={0}, to_apply=%get-tuple-element.5.reduce_sub_computation | reduce | bytes 3076 | tf_op jit(solution)/shard_map/correlate/pallas_call | solution.py:591
